TPU v7x, 32 devices: a whole 2x2x4 slice. The times are simulated.
32 devices in a mesh: blk: 4 (over y, core), rep: 8 (over z, x).
Axes of the slice: x: 2, y: 2, z: 4, core: 2. Of those that a mesh axis runs over, the one named last changes fastest.
Arguments:
- grad_out: bfloat16 [4096, 256], P(('blk', 'rep')), may hold values from -6 to 6
- relu_bits: int32 [4096, 256], P(('blk', 'rep')), may hold values 0 or 1
- features: bfloat16 [4096, 256], P(('blk', 'rep')), may hold values from -6 to 6
- weight: bfloat16 [256, 256], replicated, may hold values from -0.375 to 0.375
- tiles: bfloat16 [32, 4, 2, 128, 128], P(('blk', 'rep')), as said below
- tile_rows: int32 [32, 4, 2], P(('blk', 'rep')), may hold values from 0 to 7
- tile_counts: int32 [32, 4], P(('blk', 'rep')), may hold values from 1 to 2, as said below
Outputs:
- grad_features: bfloat16 [4096, 256], P(('blk', 'rep'))
- grad_weight: float32 [256, 256], replicated
Inputs may be any that keep to these rules, and one draw needn't show every extreme that they name: `tile_counts`: for every sub-block, some source block has exactly 2 nonzero tiles; loads differ between sub-blocks. `tiles`: about one entry in eight of a tile is nonzero.
All inputs are finite; a program needn't handle non-finite values. No bound on the sum of `relu_bits` on one device may be relied on, other than what follows from the above.
Results may differ from a plain program's by a relative error of at most 0.005.
Values may be sent and summed in bfloat16 or wider, within the bound.
A program may use at most 64 MiB of HBM per device.

v0:
```python
import jax
import jax.numpy as jnp
from jax import lax
from jax.sharding import PartitionSpec as P


def from_behind(array, axis, by):
    devices = lax.axis_size(axis)
    return lax.ppermute(array, axis, [(i, (i + by) % devices) for i in range(devices)])


def body(grad_out, relu_bits, features, weight, tiles, tile_rows, tile_counts):
    nblk = lax.axis_size("blk")
    nrep = lax.axis_size("rep")
    my_block = lax.axis_index("blk")
    rows_here = grad_out.shape[0]
    width = grad_out.shape[1]
    tile_height = tiles.shape[4]
    slot_count = tiles.shape[2]
    block_tiles = rows_here * nrep // tile_height
    masked = jnp.where(relu_bits == 1, grad_out, jnp.zeros_like(grad_out))
    slots = jnp.arange(slot_count, dtype=jnp.int32)
    my_tiles = tiles[0]
    my_rows = tile_rows[0]
    my_counts = tile_counts[0]

    def accumulate(partial_value, piece, source):
        tile_set = lax.dynamic_index_in_dim(my_tiles, source, 0, keepdims=False)
        rows_set = lax.dynamic_index_in_dim(my_rows, source, 0, keepdims=False)
        count = lax.dynamic_index_in_dim(my_counts, source, 0, keepdims=False)
        prods = jnp.einsum("krt,rf->ktf", tile_set, piece, preferred_element_type=jnp.float32)
        live = (slots < count)[:, None, None]
        prods = jnp.where(live, prods, jnp.zeros_like(prods))
        return partial_value.at[rows_set].add(prods)

    partial_value = jnp.zeros((block_tiles, tile_height, width), jnp.float32)
    partial_value = accumulate(partial_value, masked, my_block)

    def one_turn(turn, carry):
        partial_value, held = carry
        held = from_behind(held, "blk", 1)
        source = (my_block - turn) % nblk
        return (accumulate(partial_value, held, source), held)

    partial_value, held = lax.fori_loop(1, nblk, one_turn, (partial_value, masked))
    summed = lax.psum_scatter(
        partial_value.reshape(block_tiles * tile_height, width),
        "rep",
        scatter_dimension=0,
        tiled=True,
    )
    aggregated = summed.astype(jnp.bfloat16)
    grad_features = lax.dot_general(
        aggregated, weight, (((1,), (1,)), ((), ())), preferred_element_type=jnp.float32
    ).astype(jnp.bfloat16)
    weight_term = lax.dot_general(
        features, aggregated, (((0,), (0,)), ((), ())), preferred_element_type=jnp.float32
    )
    total_nodes = rows_here * nrep * nblk
    grad_weight = lax.psum(weight_term, ("blk", "rep")) * total_nodes ** (-0.5)
    return (grad_features, grad_weight)


def solution(mesh):
    return jax.shard_map(
        body,
        mesh=mesh,
        in_specs=(
            P(("blk", "rep"), None),
            P(("blk", "rep"), None),
            P(("blk", "rep"), None),
            P(),
            P(("blk", "rep"), None, None, None, None),
            P(("blk", "rep"), None, None),
            P(("blk", "rep"), None),
        ),
        out_specs=(P(("blk", "rep"), None), P()),
        check_vma=False,
    )
```

profile of v0, /device:TPU:0, one launch (start us, length us, event | category | flops | bytes accessed | tf_op | source)
XLA Modules:
  0.0 233.4 jit_solution(499865236234513302)
XLA Ops:
  7.2 0.7 copy-done.7
  8.5 0.7 iota_compare_fusion.1
  9.5 1.2 copy.10
  10.7 1.0 convolution_select_fusion.1
  11.8 0.7 scatter_fusion.1
  12.5 14.6 %while.18 = (s32[]{:T(128)}, f32[8,128,256]{2,1,0:T(8,128)S(1)}, bf16[128,256]{1,0:T(8,128)(2,1)S(1)}, s32[]{:T(128)}, s32[4,2]{1,0:T(4,128)S(1)}, /*index=5*/s3...) while((s32[]{:T(128)}, f32[8,128,256]{2,1,0:T(8,128)S(1)}, ...), condition=%wide.region_3.4_spmd.clone, body=%wide.region_1.3_spmd.clone.sunk | while | flops 16908312 | bytes 1573730 | solution.py:45
  13.1 0.6 dynamic_slice.64
  13.7 0.6 iota_compare_fusion.3
  14.3 2.6 %collective-permute-done = bf16[128,256]{1,0:T(8,128)(2,1)S(1)} collective-permute-done((bf16[128,256]{1,0:T(8,128)(2,1)S(1)}, bf16[128,256]{1,0:T(8,128)(2,1)S(1)}, u32[]{:S(2)}, u32[]{:S(2)}) %collective-permute-start) | collective-permute-done | bytes 65568 | tf_op jit(solution)/shard_map/while/body/eval_jaxpr/ppermute | solution.py:9
  17.1 0.7 scatter_fusion
  18.6 0.6 iota_compare_fusion.3
  19.3 2.4 %collective-permute-done = bf16[128,256]{1,0:T(8,128)(2,1)S(1)} collective-permute-done((bf16[128,256]{1,0:T(8,128)(2,1)S(1)}, bf16[128,256]{1,0:T(8,128)(2,1)S(1)}, u32[]{:S(2)}, u32[]{:S(2)}) %collective-permute-start) | collective-permute-done | bytes 65568 | tf_op jit(solution)/shard_map/while/body/eval_jaxpr/ppermute | solution.py:9
  21.8 0.7 scatter_fusion
  23.2 0.6 iota_compare_fusion.3
  23.9 2.4 %collective-permute-done = bf16[128,256]{1,0:T(8,128)(2,1)S(1)} collective-permute-done((bf16[128,256]{1,0:T(8,128)(2,1)S(1)}, bf16[128,256]{1,0:T(8,128)(2,1)S(1)}, u32[]{:S(2)}, u32[]{:S(2)}) %collective-permute-start) | collective-permute-done | bytes 65568 | tf_op jit(solution)/shard_map/while/body/eval_jaxpr/ppermute | solution.py:9
  26.4 0.7 scatter_fusion
  27.2 1.0 copy-done.1
  28.2 65.5 %reduce-scatter.2.cloned.1.call-done = f32[128,256]{1,0:T(8,128)} async-done(((f32[1024,256]{1,0:T(8,128)}), f32[128,256]{1,0:T(8,128)}) %reduce-scatter.2.cloned.1.call-update) | async-done | bytes 131088 | tf_op jit(solution)/shard_map/reduce_scatter | solution.py:46
  93.8 1.8 convolution_bitcast_fusion
  95.6 0.9 copy-done.2
  96.5 0.8 convolution_convert_fusion
  97.3 127.4 %all-reduce.2.cloned.1.call-done = f32[256,256]{0,1:T(8,128)} async-done(((f32[256,256]{0,1:T(8,128)}), f32[256,256]{0,1:T(8,128)}) %all-reduce.2.cloned.1.call-update) | async-done | bytes 262160 | tf_op jit(solution)/shard_map/psum | solution.py:60
  224.7 1.0 broadcast_multiply_fusion
  225.7 0.8 copy.12
  (37 shorter events, 3.6 us)
Async XLA Ops:
  7.2 88.4 %copy-start = (bf16[256,256]{1,0:T(8,128)(2,1)S(1)}, bf16[256,256]{1,0:T(8,128)(2,1)}, u32[]{:S(2)}) copy-start(bf16[256,256]{1,0:T(8,128)(2,1)} %param.12) | copy-start | bytes 393220
  7.2 86.6 %reduce-scatter.2.cloned.1.call-start = ((), (), s32[]{:S(2)}) async-start(), calls=%async_computation.1 | async-start | bytes 1179648 | tf_op jit(solution)/shard_map/reduce_scatter | solution.py:46
  7.2 0.7 copy-start.7
  8.5 0.7 copy-start.6
  9.5 1.2 copy-start.3
  9.5 1.2 copy-start.5
  12.6 4.4 %collective-permute-start = (bf16[128,256]{1,0:T(8,128)(2,1)S(1)}, bf16[128,256]{1,0:T(8,128)(2,1)S(1)}, u32[]{:S(2)}, u32[]{:S(2)}) collective-permute-start(bf16[128,256]{1,0:T(8,128)(2,1)S(1)} %get-tuple-element.297), channel_id=1, source_target_pairs={{0,8},{8,16},{16,24},{24,0},{1,9},{9,17},{17,25},{25,1},{2,10},{10... | collective-permute-start | bytes 196616 | tf_op jit(solution)/shard_map/while/body/eval_jaxpr/ppermute | solution.py:9
  17.9 3.7 %collective-permute-start = (bf16[128,256]{1,0:T(8,128)(2,1)S(1)}, bf16[128,256]{1,0:T(8,128)(2,1)S(1)}, u32[]{:S(2)}, u32[]{:S(2)}) collective-permute-start(bf16[128,256]{1,0:T(8,128)(2,1)S(1)} %get-tuple-element.297), channel_id=1, source_target_pairs={{0,8},{8,16},{16,24},{24,0},{1,9},{9,17},{17,25},{25,1},{2,10},{10... | collective-permute-start | bytes 196616 | tf_op jit(solution)/shard_map/while/body/eval_jaxpr/ppermute | solution.py:9
  22.5 3.7 %collective-permute-start = (bf16[128,256]{1,0:T(8,128)(2,1)S(1)}, bf16[128,256]{1,0:T(8,128)(2,1)S(1)}, u32[]{:S(2)}, u32[]{:S(2)}) collective-permute-start(bf16[128,256]{1,0:T(8,128)(2,1)S(1)} %get-tuple-element.297), channel_id=1, source_target_pairs={{0,8},{8,16},{16,24},{24,0},{1,9},{9,17},{17,25},{25,1},{2,10},{10... | collective-permute-start | bytes 196616 | tf_op jit(solution)/shard_map/while/body/eval_jaxpr/ppermute | solution.py:9
  27.2 1.0 copy-start.1
  27.2 66.6 %copy-start.4 = (bf16[128,256]{1,0:T(8,128)(2,1)S(1)}, bf16[128,256]{1,0:T(8,128)(2,1)}, u32[]{:S(2)}) copy-start(bf16[128,256]{1,0:T(8,128)(2,1)} %param.11) | copy-start | bytes 196612
  28.2 196.6 %all-reduce.2.cloned.1.call-start = ((), (), s32[]{:S(2)}) async-start(), calls=%async_computation.2 | async-start | bytes 524288 | tf_op jit(solution)/shard_map/psum | solution.py:60
  95.6 0.9 copy-start.2
Sparse Core Ops, SparseCore 0:
  28.3 65.4 reduce-scatter.1
  100.7 123.9 all-reduce.1
where the time goes:
time: 234 us; the launch traced here: 233 us
  waiting for transfers between devices  200 us (85%)
  between operations  14.2 us (6%)
  local copies, waits for them, and re-layouts  7.35 us (3%)
  other arithmetic  6.37 us (3%)
  matrix products  4.2 us (2%)
    psum x1, waiting for transfers between devices, body(): grad_weight = lax.psum(weight_term, ('blk', 'rep')) * total_nodes ** (-0.5)  127 us
    reduce_scatter x1, waiting for transfers between devices, body(): lax.psum_scatter(partial_value.reshape(block_tiles * tile_height, width),...  65.5 us
    ppermute x3, waiting for transfers between devices, from_behind(): lax.ppermute(array, axis, [(i, (i + by) % devices) for i in range(devices)])  7.38 us
  transfers between devices with their start and end apart: 5, of which 5 were waited for; matrix products, arithmetic and copies ran while one was open for 2% of the time, Pallas kernels for 0%

commit v1 on v0

--- a/solution.py
+++ b/solution.py
@@ -57,7 +57,9 @@
         features, aggregated, (((0,), (0,)), ((), ())), preferred_element_type=jnp.float32
     )
     total_nodes = rows_here * nrep * nblk
-    grad_weight = lax.psum(weight_term, ("blk", "rep")) * total_nodes ** (-0.5)
+    grad_weight = jnp.sum(lax.all_gather(weight_term, ("blk", "rep")), axis=0) * total_nodes ** (
+        -0.5
+    )
     return (grad_features, grad_weight)
 
 

time: 234 us -> 201 us (0.86)
  waiting for transfers between devices: 200 us -> 154 us
  local copies, waits for them, and re-layouts: 7.35 us -> 16.8 us
    psum x1 -> x0, waiting for transfers between devices: 127 us -> none  [body(): grad_weight = lax.psum(weight_term, ('blk', 'rep')) * total_nodes ** (-0.5)]
    all_gather x0 -> x1, waiting for transfers between devices: none -> 83.9 us  [body(): lax.all_gather(weight_term, ('blk', 'rep'))]
    unnamed x19 -> x10, local copies, waits for them, and re-layouts: 4.64 us -> 10.6 us
    ppermute x3, waiting for transfers between devices: 7.38 us -> 3.66 us  [from_behind(): lax.ppermute(array, axis, [(i, (i + by) % devices) for i in range(devices)])]
    dynamic_slice x4, local copies, waits for them, and re-layouts: 2.43 us -> 5.3 us  [accumulate(): count = lax.dynamic_index_in_dim(my_counts, source, 0, keepdims=False)]
  transfers between devices with their start and end apart: 5 -> 5, of which waited for: 5 -> 5; matrix products, arithmetic and copies ran while one was open for 2% -> 4% of each run, Pallas kernels for 0% -> 0%
where the time goes in v1:
time: 201 us
  waiting for transfers between devices  154 us (77%)
  local copies, waits for them, and re-layouts  16.8 us (8%)
  between operations  14.1 us (7%)
  other arithmetic  8.5 us (4%)
  matrix products  5.1 us (3%)
  starting transfers between devices  2.21 us (1%)
    all_gather x1, waiting for transfers between devices, body(): lax.all_gather(weight_term, ('blk', 'rep'))  83.9 us
    reduce_scatter x1, waiting for transfers between devices, body(): lax.psum_scatter(partial_value.reshape(block_tiles * tile_height, width),...  66.1 us
    unnamed x10, local copies, waits for them, and re-layouts  10.6 us
    dynamic_slice x4, local copies, waits for them, and re-layouts, accumulate(): count = lax.dynamic_index_in_dim(my_counts, source, 0, keepdims=False)  5.3 us
  transfers between devices with their start and end apart: 5, of which 5 were waited for; matrix products, arithmetic and copies ran while one was open for 4% of the time, Pallas kernels for 0%

profile of v1, /device:TPU:0, one launch (start us, length us, event | category | flops | bytes accessed | tf_op | source)
XLA Modules:
  0.0 200.6 jit_solution(3365789390521299628)
XLA Ops:
  7.2 1.4 constant_dynamic-slice_fusion
  9.3 0.9 dynamic-slice_reduce_fusion
  10.2 0.8 copy.14
  10.9 1.1 copy.13
  12.1 1.0 compare_select_fusion.1
  13.0 1.0 convolution_select_fusion.1
  14.2 0.7 scatter_fusion.1
  14.9 14.6 %while.18 = (s32[]{:T(128)}, f32[8,128,256]{2,1,0:T(8,128)S(1)}, bf16[128,256]{1,0:T(8,128)(2,1)S(1)}, s32[]{:T(128)}, s32[4,2]{1,0:T(4,128)S(1)}, /*index=5*/s3...) while((s32[]{:T(128)}, f32[8,128,256]{2,1,0:T(8,128)S(1)}, ...), condition=%wide.region_3.4_spmd.clone, body=%wide.region_1.3_spmd.clone.sunk | while | flops 16908312 | bytes 1573730 | solution.py:45
  15.4 1.3 dynamic_slice.64
  17.4 1.9 collective-permute-done
  20.2 0.8 collective-permute-start
  21.0 1.3 dynamic_slice.64
  23.1 0.9 collective-permute-done
  24.8 0.8 collective-permute-start
  25.7 1.3 dynamic_slice.64
  27.7 0.9 collective-permute-done
  29.5 1.0 copy-done.1
  30.5 66.1 %reduce-scatter.2.cloned.1.call-done = f32[128,256]{1,0:T(8,128)} async-done(((f32[1024,256]{1,0:T(8,128)}), f32[128,256]{1,0:T(8,128)}) %reduce-scatter.2.cloned.1.call-update) | async-done | bytes 131088 | tf_op jit(solution)/shard_map/reduce_scatter | solution.py:46
  96.6 1.8 convolution_bitcast_fusion
  98.5 1.7 convolution_convert_fusion
  100.2 83.9 %all-gather.3.cloned.1.call-done = f32[8192,256]{0,1:T(8,128)} async-done(((f32[256,256]{0,1:T(8,128)}), f32[8192,256]{0,1:T(8,128)}) %all-gather.3.cloned.1.call-update) | async-done | bytes 8388624 | tf_op jit(solution)/shard_map/all_gather | solution.py:60
  184.1 6.8 %copy.16 = f32[32,8,32,256]{3,2,1,0:T(8,128)S(1)} copy(f32[32,8,32,256]{3,1,2,0:T(8,128)} %bitcast.47) | data formatting | bytes 16777216
  190.9 1.9 bitcast_reduce_fusion
  192.9 0.8 copy.15
  (29 shorter events, 6.1 us)
Async XLA Ops:
  7.2 91.3 %copy-start = (bf16[256,256]{1,0:T(8,128)(2,1)S(1)}, bf16[256,256]{1,0:T(8,128)(2,1)}, u32[]{:S(2)}) copy-start(bf16[256,256]{1,0:T(8,128)(2,1)} %param.12) | copy-start | bytes 393220
  7.2 89.4 %copy-start.2 = (bf16[128,256]{1,0:T(8,128)(2,1)S(1)}, bf16[128,256]{1,0:T(8,128)(2,1)}, u32[]{:S(2)}) copy-start(bf16[128,256]{1,0:T(8,128)(2,1)} %param.11) | copy-start | bytes 196612
  7.2 89.4 %reduce-scatter.2.cloned.1.call-start = ((), (), s32[]{:S(2)}) async-start(), calls=%async_computation.1 | async-start | bytes 1179648 | tf_op jit(solution)/shard_map/reduce_scatter | solution.py:46
  14.9 4.4 %collective-permute-start = (bf16[128,256]{1,0:T(8,128)(2,1)S(1)}, bf16[128,256]{1,0:T(8,128)(2,1)S(1)}, u32[]{:S(2)}, u32[]{:S(2)}) collective-permute-start(bf16[128,256]{1,0:T(8,128)(2,1)S(1)} %get-tuple-element.304), channel_id=1, source_target_pairs={{0,8},{8,16},{16,24},{24,0},{1,9},{9,17},{17,25},{25,1},{2,10},{10... | collective-permute-start | bytes 196616 | tf_op jit(solution)/shard_map/while/body/eval_jaxpr/ppermute | solution.py:9
  20.2 3.7 %collective-permute-start = (bf16[128,256]{1,0:T(8,128)(2,1)S(1)}, bf16[128,256]{1,0:T(8,128)(2,1)S(1)}, u32[]{:S(2)}, u32[]{:S(2)}) collective-permute-start(bf16[128,256]{1,0:T(8,128)(2,1)S(1)} %get-tuple-element.304), channel_id=1, source_target_pairs={{0,8},{8,16},{16,24},{24,0},{1,9},{9,17},{17,25},{25,1},{2,10},{10... | collective-permute-start | bytes 196616 | tf_op jit(solution)/shard_map/while/body/eval_jaxpr/ppermute | solution.py:9
  24.8 3.7 %collective-permute-start = (bf16[128,256]{1,0:T(8,128)(2,1)S(1)}, bf16[128,256]{1,0:T(8,128)(2,1)S(1)}, u32[]{:S(2)}, u32[]{:S(2)}) collective-permute-start(bf16[128,256]{1,0:T(8,128)(2,1)S(1)} %get-tuple-element.304), channel_id=1, source_target_pairs={{0,8},{8,16},{16,24},{24,0},{1,9},{9,17},{17,25},{25,1},{2,10},{10... | collective-permute-start | bytes 196616 | tf_op jit(solution)/shard_map/while/body/eval_jaxpr/ppermute | solution.py:9
  29.5 1.0 copy-start.1
  30.5 153.6 %all-gather.3.cloned.1.call-start = ((), (), s32[]{:S(2)}) async-start(), calls=%async_computation.2 | async-start | bytes 8650752 | tf_op jit(solution)/shard_map/all_gather | solution.py:60
Sparse Core Ops, SparseCore 0:
  30.6 65.9 reduce-scatter.1
  100.5 83.5 all-gather.2

commit v2 on v0

--- a/solution.py
+++ b/solution.py
@@ -57,7 +57,7 @@
         features, aggregated, (((0,), (0,)), ((), ())), preferred_element_type=jnp.float32
     )
     total_nodes = rows_here * nrep * nblk
-    grad_weight = lax.psum(weight_term, ("blk", "rep")) * total_nodes ** (-0.5)
+    grad_weight = lax.psum(lax.psum(weight_term, "rep"), "blk") * total_nodes ** (-0.5)
     return (grad_features, grad_weight)
 
 

time: 234 us -> 210 us (0.90)
  waiting for transfers between devices: 200 us -> 177 us
    psum x1 -> x2, waiting for transfers between devices: 127 us -> 104 us  [the longest x1 72 us: body(): lax.psum(weight_term, 'rep')]
  transfers between devices with their start and end apart: 5 -> 6, of which waited for: 5 -> 6; matrix products, arithmetic and copies ran while one was open for 2% -> 2% of each run, Pallas kernels for 0% -> 0%
where the time goes in v2:
time: 210 us
  waiting for transfers between devices  177 us (84%)
  between operations  13.9 us (7%)
  local copies, waits for them, and re-layouts  7.35 us (4%)
  other arithmetic  6.37 us (3%)
  matrix products  4.19 us (2%)
    psum x1, waiting for transfers between devices, body(): lax.psum(weight_term, 'rep')  72 us
    reduce_scatter x1, waiting for transfers between devices, body(): lax.psum_scatter(partial_value.reshape(block_tiles * tile_height, width),...  65.5 us
    psum x1, waiting for transfers between devices, body(): lax.psum(lax.psum(weight_term, 'rep'), 'blk') * total_nodes ** (-0.5)  31.9 us
    ppermute x3, waiting for transfers between devices, from_behind(): lax.ppermute(array, axis, [(i, (i + by) % devices) for i in range(devices)])  7.38 us
    unnamed x19, local copies, waits for them, and re-layouts  4.64 us
  transfers between devices with their start and end apart: 6, of which 6 were waited for; matrix products, arithmetic and copies ran while one was open for 2% of the time, Pallas kernels for 0%

profile of v2, /device:TPU:0, one launch (start us, length us, event | category | flops | bytes accessed | tf_op | source)
XLA Modules:
  0.0 209.6 jit_solution(7709253824193592484)
XLA Ops:
  7.2 0.7 copy-done.7
  8.5 0.7 iota_compare_fusion.1
  9.5 1.2 copy.10
  10.7 1.0 convolution_select_fusion.1
  11.8 0.7 scatter_fusion.1
  12.5 14.6 %while.18 = (s32[]{:T(128)}, f32[8,128,256]{2,1,0:T(8,128)S(1)}, bf16[128,256]{1,0:T(8,128)(2,1)S(1)}, s32[]{:T(128)}, s32[4,2]{1,0:T(4,128)S(1)}, /*index=5*/s3...) while((s32[]{:T(128)}, f32[8,128,256]{2,1,0:T(8,128)S(1)}, ...), condition=%wide.region_3.4_spmd.clone, body=%wide.region_1.3_spmd.clone.sunk | while | flops 16908312 | bytes 1573730 | solution.py:45
  13.7 0.6 iota_compare_fusion.3
  14.3 2.6 %collective-permute-done = bf16[128,256]{1,0:T(8,128)(2,1)S(1)} collective-permute-done((bf16[128,256]{1,0:T(8,128)(2,1)S(1)}, bf16[128,256]{1,0:T(8,128)(2,1)S(1)}, u32[]{:S(2)}, u32[]{:S(2)}) %collective-permute-start) | collective-permute-done | bytes 65568 | tf_op jit(solution)/shard_map/while/body/eval_jaxpr/ppermute | solution.py:9
  17.1 0.7 scatter_fusion
  18.6 0.6 iota_compare_fusion.3
  19.3 2.4 %collective-permute-done = bf16[128,256]{1,0:T(8,128)(2,1)S(1)} collective-permute-done((bf16[128,256]{1,0:T(8,128)(2,1)S(1)}, bf16[128,256]{1,0:T(8,128)(2,1)S(1)}, u32[]{:S(2)}, u32[]{:S(2)}) %collective-permute-start) | collective-permute-done | bytes 65568 | tf_op jit(solution)/shard_map/while/body/eval_jaxpr/ppermute | solution.py:9
  21.8 0.7 scatter_fusion
  23.2 0.6 iota_compare_fusion.3
  23.9 2.4 %collective-permute-done = bf16[128,256]{1,0:T(8,128)(2,1)S(1)} collective-permute-done((bf16[128,256]{1,0:T(8,128)(2,1)S(1)}, bf16[128,256]{1,0:T(8,128)(2,1)S(1)}, u32[]{:S(2)}, u32[]{:S(2)}) %collective-permute-start) | collective-permute-done | bytes 65568 | tf_op jit(solution)/shard_map/while/body/eval_jaxpr/ppermute | solution.py:9
  26.4 0.7 scatter_fusion
  27.2 1.0 copy-done.1
  28.2 65.5 %reduce-scatter.2.cloned.1.call-done = f32[128,256]{1,0:T(8,128)} async-done(((f32[1024,256]{1,0:T(8,128)}), f32[128,256]{1,0:T(8,128)}) %reduce-scatter.2.cloned.1.call-update) | async-done | bytes 131088 | tf_op jit(solution)/shard_map/reduce_scatter | solution.py:46
  93.8 1.8 convolution_bitcast_fusion
  95.7 72.0 %all-reduce.3.cloned.1.call-done = f32[256,256]{0,1:T(8,128)} async-done(((f32[256,256]{0,1:T(8,128)}), f32[256,256]{0,1:T(8,128)}) %all-reduce.3.cloned.1.call-update) | async-done | bytes 262160 | tf_op jit(solution)/shard_map/psum | solution.py:60
  167.7 0.9 copy-done.2
  168.6 0.8 convolution_convert_fusion
  169.4 31.9 %all-reduce.5.cloned.1.call-done = f32[256,256]{0,1:T(8,128)} async-done(((f32[256,256]{0,1:T(8,128)}), f32[256,256]{0,1:T(8,128)}) %all-reduce.5.cloned.1.call-update) | async-done | bytes 262160 | tf_op jit(solution)/shard_map/psum | solution.py:60
  201.3 1.0 broadcast_multiply_fusion
  202.3 0.8 copy.12
  (40 shorter events, 4.3 us)
Async XLA Ops:
  7.2 160.5 %copy-start = (bf16[256,256]{1,0:T(8,128)(2,1)S(1)}, bf16[256,256]{1,0:T(8,128)(2,1)}, u32[]{:S(2)}) copy-start(bf16[256,256]{1,0:T(8,128)(2,1)} %param.12) | copy-start | bytes 393220
  7.2 86.6 %reduce-scatter.2.cloned.1.call-start = ((), (), s32[]{:S(2)}) async-start(), calls=%async_computation.1 | async-start | bytes 1179648 | tf_op jit(solution)/shard_map/reduce_scatter | solution.py:46
  7.2 0.7 copy-start.7
  8.5 0.7 copy-start.6
  9.5 1.2 copy-start.3
  9.5 1.2 copy-start.5
  12.6 4.4 %collective-permute-start = (bf16[128,256]{1,0:T(8,128)(2,1)S(1)}, bf16[128,256]{1,0:T(8,128)(2,1)S(1)}, u32[]{:S(2)}, u32[]{:S(2)}) collective-permute-start(bf16[128,256]{1,0:T(8,128)(2,1)S(1)} %get-tuple-element.297), channel_id=1, source_target_pairs={{0,8},{8,16},{16,24},{24,0},{1,9},{9,17},{17,25},{25,1},{2,10},{10... | collective-permute-start | bytes 196616 | tf_op jit(solution)/shard_map/while/body/eval_jaxpr/ppermute | solution.py:9
  17.9 3.7 %collective-permute-start = (bf16[128,256]{1,0:T(8,128)(2,1)S(1)}, bf16[128,256]{1,0:T(8,128)(2,1)S(1)}, u32[]{:S(2)}, u32[]{:S(2)}) collective-permute-start(bf16[128,256]{1,0:T(8,128)(2,1)S(1)} %get-tuple-element.297), channel_id=1, source_target_pairs={{0,8},{8,16},{16,24},{24,0},{1,9},{9,17},{17,25},{25,1},{2,10},{10... | collective-permute-start | bytes 196616 | tf_op jit(solution)/shard_map/while/body/eval_jaxpr/ppermute | solution.py:9
  22.5 3.7 %collective-permute-start = (bf16[128,256]{1,0:T(8,128)(2,1)S(1)}, bf16[128,256]{1,0:T(8,128)(2,1)S(1)}, u32[]{:S(2)}, u32[]{:S(2)}) collective-permute-start(bf16[128,256]{1,0:T(8,128)(2,1)S(1)} %get-tuple-element.297), channel_id=1, source_target_pairs={{0,8},{8,16},{16,24},{24,0},{1,9},{9,17},{17,25},{25,1},{2,10},{10... | collective-permute-start | bytes 196616 | tf_op jit(solution)/shard_map/while/body/eval_jaxpr/ppermute | solution.py:9
  27.2 1.0 copy-start.1
  27.2 66.6 %copy-start.4 = (bf16[128,256]{1,0:T(8,128)(2,1)S(1)}, bf16[128,256]{1,0:T(8,128)(2,1)}, u32[]{:S(2)}) copy-start(bf16[128,256]{1,0:T(8,128)(2,1)} %param.11) | copy-start | bytes 196612
  28.2 139.5 %all-reduce.3.cloned.1.call-start = ((), (), s32[]{:S(2)}) async-start(), calls=%async_computation.2 | async-start | bytes 524288 | tf_op jit(solution)/shard_map/psum | solution.py:60
  95.6 105.7 %all-reduce.5.cloned.1.call-start = ((), (), s32[]{:S(2)}) async-start(), calls=%async_computation.3 | async-start | bytes 524288 | tf_op jit(solution)/shard_map/psum | solution.py:60
  167.7 0.9 copy-start.2
Sparse Core Ops, SparseCore 0:
  28.3 65.4 reduce-scatter.1
  98.1 69.5 all-reduce.2
  170.0 31.2 all-reduce.4
